TPU v7x, 32 devices: a whole 2x2x4 slice. The times are simulated.
32 devices in a mesh: coord: 8 (over z, x), dp: 4 (over y, core).
Axes of the slice: x: 2, y: 2, z: 4, core: 2. Of those that a mesh axis runs over, the one named last changes fastest.
Arguments:
- h_train: bfloat16 [2, 512, 256, 128], P(None, 'dp'), may hold values from -6 to 6
- gout_train: bfloat16 [2, 512, 256, 5120], P(None, 'dp', None, 'coord'), may hold values from -96 to 96
- h_val: bfloat16 [2, 64, 256, 128], P(None, 'dp'), may hold values from -6 to 6
- gout_val: bfloat16 [2, 64, 256, 5120], P(None, 'dp', None, 'coord'), may hold values from -96 to 96
- proj: bfloat16 [2, 5120, 128, 128], P(None, 'coord'), may hold values from -0.0390625 to 0.0390625
- bins: int32 [2, 5120], P(None, 'coord'), may hold values from 0 to 63
- tasks: int32 [64, 1], replicated, may hold values from 0 to 2
Outputs:
- cosines: float32 [512, 64], P('dp')
- scores: float32 [512, 3], P('dp')
Inputs may be any that keep to these rules, and one draw needn't show every extreme that they name: `tasks`: every one of the 3 benchmarks has at least one validation example.
All inputs are finite; a program needn't handle non-finite values.
Results may differ from a plain program's by a relative error of at most 0.0003.
Values sent between devices are 32-bit elements; how exact they have to be, the bound alone decides.
A program may use at most 384 MiB of HBM per device.

v0:
```python
import jax
import jax.numpy as jnp
from jax import lax
from jax.sharding import PartitionSpec as P

KPROJ = 8192
BW = 128
NTASK = 3


def local_features(h_all, g_all, proj, bins):
    block_count = KPROJ // BW
    total = jnp.zeros((h_all.shape[1], block_count, BW), jnp.float32)
    for layer in range(h_all.shape[0]):
        grads = jnp.einsum(
            "etr,etj->ejr", h_all[layer], g_all[layer], preferred_element_type=jnp.float32
        ).astype(jnp.bfloat16)
        placed = jnp.einsum("ejr,jrk->ejk", grads, proj[layer], preferred_element_type=jnp.float32)
        onehot = (bins[layer][:, None] == jnp.arange(block_count)[None, :]).astype(jnp.float32)
        total = total + jnp.einsum("ejk,jb->ebk", placed, onehot, precision=lax.Precision.HIGHEST)
    return total.reshape(h_all.shape[1], block_count * BW)


def task_means(cosines, tasks):
    members = (tasks[:, 0][:, None] == jnp.arange(NTASK)[None, :]).astype(jnp.float32)
    return (
        jnp.dot(cosines, members, precision=lax.Precision.HIGHEST)
        / jnp.sum(members, axis=0)[None, :]
    )


def per_device(h_train, gout_train, h_val, gout_val, proj, bins, tasks):
    train_terms = local_features(h_train, gout_train, proj, bins)
    val_terms = local_features(h_val, gout_val, proj, bins)
    train_feats, val_local = lax.psum((train_terms, val_terms), "coord")
    val_feats = lax.all_gather(val_local, "dp", axis=0, tiled=True)
    train_norm = jnp.sqrt(jnp.sum(train_feats * train_feats, axis=1) + 1e-06)
    val_norm = jnp.sqrt(jnp.sum(val_feats * val_feats, axis=1) + 1e-06)
    dots = jnp.dot(train_feats, val_feats.T, precision=lax.Precision.HIGHEST)
    cosines = dots / (train_norm[:, None] * val_norm[None, :])
    return (cosines, task_means(cosines, tasks))


def solution(mesh):
    in_specs = (
        P(None, "dp", None, None),
        P(None, "dp", None, "coord"),
        P(None, "dp", None, None),
        P(None, "dp", None, "coord"),
        P(None, "coord", None, None),
        P(None, "coord"),
        P(),
    )
    out_specs = (P("dp", None), P("dp", None))
    return jax.shard_map(
        per_device, mesh=mesh, in_specs=in_specs, out_specs=out_specs, check_vma=False
    )
```

profile of v0, /device:TPU:0, one launch (start us, length us, event | category | flops | bytes accessed | tf_op | source)
XLA Modules:
  0.0 492.4 jit_solution(6510401668994472613)
XLA Ops:
  7.2 0.0 all-reduce.3.cloned.1.call-start
  7.2 27.2 %fusion.29 = bf16[128,640,128]{2,1,0:T(8,128)(2,1)} fusion(bf16[2,128,256,640]{3,2,1,0:T(8,128)(2,1)} %param.8, bf16[2,128,256,128]{3,2,1,0:T(8,128)(2,1)} %param.7), kind=kOutput, calls=%fused_computation.27 | convolution fusion | flops 5379194880 | bytes 71303168 | tf_op jit(solution)/shard_map/etr,etj->ejr/dot_general | solution.py:15
  34.4 0.0 copy-start.3
  34.4 27.4 %fusion.26 = bf16[128,640,128]{2,1,0:T(8,128)(2,1)} fusion(bf16[2,128,256,640]{3,2,1,0:T(8,128)(2,1)} %param.8, bf16[2,128,256,128]{3,2,1,0:T(8,128)(2,1)} %param.7), kind=kOutput, calls=%fused_computation.26 | convolution fusion | flops 5379194880 | bytes 71303168 | tf_op jit(solution)/shard_map/etr,etj->ejr/dot_general | solution.py:15
  61.8 0.0 copy-done.3
  61.8 0.0 copy-start.2
  61.8 5.6 %fusion.53 = bf16[16,640,128]{2,1,0:T(8,128)(2,1)} fusion(bf16[2,16,256,640]{3,2,1,0:T(8,128)(2,1)} %param.10, bf16[2,16,256,128]{3,2,1,0:T(8,128)(2,1)S(1)} %copy-done.3), kind=kOutput, calls=%fused_computation.50 | convolution fusion | flops 672399360 | bytes 8912896 | tf_op jit(solution)/shard_map/etr,etj->ejr/dot_general | solution.py:15
  67.4 4.4 fusion.50
  71.8 0.0 copy-done.2
  71.8 36.0 %fusion.14 = f32[640,128,128]{2,1,0:T(8,128)} fusion(bf16[128,640,128]{2,1,0:T(8,128)(2,1)} %fusion.29, bf16[2,640,128,128]{3,2,1,0:T(8,128)(2,1)} %param.11), kind=kOutput, calls=%fused_computation.14 | convolution fusion | flops 2684354560 | bytes 83886080 | tf_op jit(solution)/shard_map/ejr,jrk->ejk/dot_general | solution.py:18
  107.9 35.7 %fusion.18 = f32[640,128,128]{2,1,0:T(8,128)} fusion(bf16[128,640,128]{2,1,0:T(8,128)(2,1)} %fusion.26, bf16[2,640,128,128]{3,2,1,0:T(8,128)(2,1)} %param.11), kind=kOutput, calls=%fused_computation.18 | convolution fusion | flops 2684354560 | bytes 83886080 | tf_op jit(solution)/shard_map/ejr,jrk->ejk/dot_general | solution.py:18
  143.6 49.0 %fusion = f32[64,128,128]{2,0,1:T(8,128)} fusion(f32[640,128,128]{2,1,0:T(8,128)} %fusion.14, s32[640]{0:T(1024)S(1)} %get-tuple-element.3), kind=kOutput, calls=%fused_computation | convolution fusion | flops 8053104640 | bytes 46139904 | tf_op jit(solution)/shard_map/ejk,jb->ebk/dot_general | solution.py:20
  192.6 49.4 %fusion.56 = f32[64,128,128]{2,0,1:T(8,128)} fusion(f32[64,128,128]{2,0,1:T(8,128)} %fusion, f32[640,128,128]{2,1,0:T(8,128)} %fusion.18, s32[640]{0:T(1024)S(1)} %get-tuple-element.2), kind=kOutput, calls=%fused_computation.51 | convolution fusion | flops 8054153216 | bytes 50334208 | tf_op jit(solution)/shard_map/ejk,jb->ebk/dot_general | solution.py:20
  242.0 0.0 copy-start
  242.0 7.5 %copy.49 = f32[16,8,64,128]{3,1,2,0:T(8,128)} copy(f32[16,8,64,128]{3,2,1,0:T(8,128)} %bitcast.80) | data formatting | bytes 8388608
  249.6 0.0 copy-done
  249.6 10.6 %fusion.12 = f32[640,16,128]{2,1,0:T(8,128)S(1)} fusion(bf16[2,640,128,128]{3,2,1,0:T(8,128)(2,1)} %param.11, bf16[16,640,128]{2,1,0:T(8,128)(2,1)S(1)} %copy-done), kind=kOutput, calls=%fused_computation.12 | convolution fusion | flops 335544320 | bytes 28835840 | tf_op jit(solution)/shard_map/ejr,jrk->ejk/dot_general | solution.py:18
  260.2 3.5 fusion.36
  263.6 10.9 %fusion.16 = f32[640,16,128]{2,1,0:T(8,128)S(1)} fusion(bf16[2,640,128,128]{3,2,1,0:T(8,128)(2,1)} %param.11, bf16[16,640,128]{2,1,0:T(8,128)(2,1)S(1)} %fusion.50), kind=kOutput, calls=%fused_computation.16 | convolution fusion | flops 335544320 | bytes 28835840 | tf_op jit(solution)/shard_map/ejr,jrk->ejk/dot_general | solution.py:18
  274.5 0.0 copy-start.4
  274.5 3.5 fusion.59
  278.0 1.2 copy.50
  279.2 0.0 all-reduce.3.cloned.1.call-update
  279.2 0.0 all-gather.2.cloned.1.call-start
  279.3 172.8 %all-reduce.3.cloned.1.call-done = (f32[128,8192]{1,0:T(8,128)}, f32[16,8192]{1,0:T(8,128)}) async-done(((f32[128,8192]{1,0:T(8,128)}, f32[16,8192]{1,0:T(8,128)}), (f32[128,8192]{1,0:T(8,128)}, f32[16,8192]{1,0:T(8,128)})) %all-reduce.3.cloned.1.call-update) | async-done | bytes 4718608 | tf_op jit(solution)/shard_map/psum | solution.py:35
  452.1 0.0 all-gather.2.cloned.1.call-update
  452.1 0.0 copy-done.4
  452.1 0.1 convert_reduce_fusion
  452.2 2.5 multiply_reduce_fusion
  454.8 20.5 %all-gather.2.cloned.1.call-done = f32[64,8192]{1,0:T(8,128)} async-done(((f32[16,8192]{1,0:T(8,128)}), f32[64,8192]{1,0:T(8,128)}) %all-gather.2.cloned.1.call-update) | async-done | bytes 2097168 | tf_op jit(solution)/shard_map/all_gather | solution.py:36
  475.2 1.8 multiply_reduce_fusion.1
  477.1 7.3 %convolution_divide_fusion = f32[128,64]{0,1:T(8,128)S(1)} fusion(f32[128,8192]{1,0:T(8,128)} %get-tuple-element.4, f32[64,8192]{1,0:T(8,128)} %all-gather.2.cloned.1.call-done, f32[64]{0:T(128)S(1)} %add_sqrt_fusion, f32[128]{0:T(128)S(1)} %add_sqrt_fusion.1), kind=kOutput, calls=%fused_computation.53 | convolution fusion | flops 805322752 | bytes 6324992 | tf_op jit(solution)/shard_map/dot_general | solution.py:39
  484.4 0.0 copy-start.1
  484.4 0.7 convolution_divide_fusion.1
  485.1 0.0 copy-done.1
  (3 shorter events, 0.0 us)
Async XLA Ops:
  7.2 444.9 %all-reduce.3.cloned.1.call-start = ((), (), s32[]{:S(2)}) async-start(), calls=%async_computation.1 | async-start | bytes 9437184 | tf_op jit(solution)/shard_map/psum | solution.py:35
  34.4 27.4 %copy-start.3 = (bf16[2,16,256,128]{3,2,1,0:T(8,128)(2,1)S(1)}, bf16[2,16,256,128]{3,2,1,0:T(8,128)(2,1)}, u32[]{:S(2)}) copy-start(bf16[2,16,256,128]{3,2,1,0:T(8,128)(2,1)} %param.9) | copy-start | bytes 6291460
  61.8 10.0 %copy-start.2 = (s32[2,640]{1,0:T(2,128)S(1)}, s32[2,640]{1,0:T(2,128)}, u32[]{:S(2)}) copy-start(s32[2,640]{1,0:T(2,128)} %param.12) | copy-start | bytes 15364
  242.0 7.6 %copy-start = (bf16[16,640,128]{2,1,0:T(8,128)(2,1)S(1)}, bf16[16,640,128]{2,1,0:T(8,128)(2,1)}, u32[]{:S(2)}) copy-start(bf16[16,640,128]{2,1,0:T(8,128)(2,1)} %fusion.53) | copy-start | bytes 7864324
  274.5 177.6 %copy-start.4 = (s32[64,1]{0,1:T(1,128)S(1)}, s32[64,1]{0,1:T(1,128)}, u32[]{:S(2)}) copy-start(s32[64,1]{0,1:T(1,128)} %param.13) | copy-start | bytes 772
  279.2 196.0 %all-gather.2.cloned.1.call-start = ((), (), s32[]{:S(2)}) async-start(), calls=%async_computation | async-start | bytes 2621440 | tf_op jit(solution)/shard_map/all_gather | solution.py:36
  484.4 0.7 copy-start.1
Sparse Core Ops, SparseCore 0:
  279.3 172.6 all-reduce.2
  453.6 21.5 all-gather.1
where the time goes:
time: 499 us; the launch traced here: 492 us
  matrix products  271 us (54%)
  waiting for transfers between devices  193 us (39%)
  between operations  14.6 us (3%)
  local copies, waits for them, and re-layouts  8.77 us (2%)
    psum x1, waiting for transfers between devices, per_device(): train_feats, val_local = lax.psum((train_terms, val_terms), 'coord')  173 us
    dot_general x4, matrix products, local_features(): jnp.einsum('ejk,jb->ebk', placed, onehot, precision=lax.Precision.HIGHEST)  105 us
    dot_general x4, matrix products, local_features(): jnp.einsum('ejr,jrk->ejk', grads, proj[layer], preferred_element_type=jnp...  93.2 us
    dot_general x4, matrix products, local_features(): jnp.einsum('etr,etj->ejr', h_all[layer], g_all[layer], preferred_element_...  64.6 us
    all_gather x1, waiting for transfers between devices, per_device(): val_feats = lax.all_gather(val_local, 'dp', axis=0, tiled=True)  20.5 us
  transfers between devices with their start and end apart: 2, of which 2 were waited for; matrix products, arithmetic and copies ran while one was open for 1% of the time, Pallas kernels for 0%

commit v1 on v0

v1 whole, which is shorter than its diff:
```python
import functools

import jax
import jax.numpy as jnp
from jax import lax
from jax.experimental import pallas as pl
from jax.experimental.pallas import tpu as pltpu
from jax.sharding import PartitionSpec as P

KPROJ = 8192
BW = 128
NTASK = 3
NBIN = KPROJ // BW
SUB = 8
STRIDE = SUB + 1


def features_kernel(width, n_sets, bins_ref, *refs):
    pairs = [(refs[2 * s], refs[2 * s + 1]) for s in range(n_sets)]
    proj_ref, out_ref, grads_ref = refs[2 * n_sets :]
    layer, block = pl.program_id(0), pl.program_id(1)
    n_blocks = pl.num_programs(1)
    groups = grads_ref.shape[0]

    @pl.when((layer == 0) & (block == 0))
    def _():
        out_ref[...] = jnp.zeros_like(out_ref)

    first = 0
    for g_ref, h_ref in pairs:
        n_groups = g_ref.shape[1] // SUB

        def one_group(group, carry, g_ref=g_ref, h_ref=h_ref, first=first):
            for i in range(SUB):
                e = group * SUB + i
                grads = lax.dot_general(
                    g_ref[0, e],
                    h_ref[0, e],
                    (((0,), (0,)), ((), ())),
                    preferred_element_type=jnp.float32,
                )
                for jj in range(width // SUB):
                    grads_ref[first + group, jj, pl.ds(i * STRIDE, SUB), :] = grads[
                        jj * SUB : (jj + 1) * SUB
                    ]
            return carry

        lax.fori_loop(0, n_groups, one_group, 0)
        first += n_groups

    base = (layer * n_blocks + block) * width

    def columns(jj, carry):
        placed = []
        for i in range(SUB):
            rows = jnp.concatenate(
                [grads_ref[group, jj, pl.ds(i, SUB, stride=STRIDE), :] for group in range(groups)],
                axis=0,
            ).astype(jnp.bfloat16)
            placed.append(
                jnp.dot(rows, proj_ref[0, jj * SUB + i], preferred_element_type=jnp.float32)
            )
            if len(placed) == 4:
                for k in range(4):
                    b = bins_ref[base + jj * SUB + i - 3 + k]
                    out_ref[b] += placed[k]
                placed = []
        return carry

    lax.fori_loop(0, width // SUB, columns, 0)


def features(bins, proj, sets):
    layers, columns = proj.shape[0], proj.shape[1]
    width = 128 if columns % 128 == 0 else columns
    examples = sum(size for _, _, size, _ in sets)
    in_specs, operands = [], []
    for g, h, size, at in sets:
        in_specs.append(
            pl.BlockSpec((1, size, g.shape[2], width), lambda l, j, b, at=at: (l, at, 0, j))
        )
        in_specs.append(
            pl.BlockSpec((1, size, h.shape[2], h.shape[3]), lambda l, j, b, at=at: (l, at, 0, 0))
        )
        operands += [g, h]
    in_specs.append(
        pl.BlockSpec((1, width, proj.shape[2], BW), lambda l, j, b: (l, j, 0, 0))
    )
    tok, rank = sets[0][1].shape[2:]
    flops = 2 * layers * examples * columns * rank * (tok + BW)
    moved = 2 * layers * (examples * tok * (columns + rank) + columns * rank * BW)
    return pl.pallas_call(
        functools.partial(features_kernel, width, len(sets)),
        grid_spec=pltpu.PrefetchScalarGridSpec(
            num_scalar_prefetch=1,
            grid=(layers, columns // width),
            in_specs=in_specs,
            out_specs=pl.BlockSpec((NBIN, examples, BW), lambda l, j, b: (0, 0, 0)),
            scratch_shapes=[
                pltpu.VMEM((examples // SUB, width // SUB, SUB * STRIDE, rank), jnp.float32)
            ],
        ),
        out_shape=jax.ShapeDtypeStruct((NBIN, examples, BW), jnp.float32),
        compiler_params=pltpu.CompilerParams(
            dimension_semantics=("arbitrary", "arbitrary"), vmem_limit_bytes=60 * 1024 * 1024
        ),
        cost_estimate=pl.CostEstimate(flops=flops, bytes_accessed=moved, transcendentals=0),
    )(bins.reshape(-1), *operands, proj)


def per_device(h_train, gout_train, h_val, gout_val, proj, bins, tasks):
    n_train, n_val = h_train.shape[1], h_val.shape[1]
    half = n_train // 2
    first = features(
        bins, proj, [(gout_train, h_train, half, 0), (gout_val, h_val, n_val, 0)]
    )
    second = features(bins, proj, [(gout_train, h_train, half, 1)])
    first = lax.psum_scatter(first, "coord", scatter_dimension=0, tiled=True)
    second = lax.psum_scatter(second, "coord", scatter_dimension=0, tiled=True)
    val = lax.all_gather(first[:, half:], "dp", axis=1, tiled=True)

    def against(rows):
        dots = jnp.einsum("bek,bvk->ev", rows, val, precision=lax.Precision.HIGHEST)
        return dots, jnp.sum(rows * rows, axis=(0, 2))

    parts = [against(first[:, :half]), against(second)]
    val_sq = jnp.sum(val * val, axis=(0, 2))
    dots = jnp.concatenate([p[0] for p in parts], axis=0)
    train_sq = jnp.concatenate([p[1] for p in parts], axis=0)
    dots, train_sq, val_sq = lax.psum((dots, train_sq, val_sq), "coord")
    train_norm = jnp.sqrt(train_sq + 1e-06)
    val_norm = jnp.sqrt(val_sq + 1e-06)
    cosines = dots / (train_norm[:, None] * val_norm[None, :])
    members = (tasks[:, 0][:, None] == jnp.arange(NTASK)[None, :]).astype(jnp.float32)
    scores = (
        jnp.dot(cosines, members, precision=lax.Precision.HIGHEST)
        / jnp.sum(members, axis=0)[None, :]
    )
    return (cosines, scores)


def solution(mesh):
    in_specs = (
        P(None, "dp", None, None),
        P(None, "dp", None, "coord"),
        P(None, "dp", None, None),
        P(None, "dp", None, "coord"),
        P(None, "coord", None, None),
        P(None, "coord"),
        P(),
    )
    out_specs = (P("dp", None), P("dp", None))
    return jax.shard_map(
        per_device, mesh=mesh, in_specs=in_specs, out_specs=out_specs, check_vma=False
    )
```

time: 499 us -> 287 us (0.58); the launches traced: 492 us -> 286 us
  matrix products: 271 us -> 3.34 us
  Pallas kernels: 0 us -> 151 us
  waiting for transfers between devices: 193 us -> 72.1 us
  blocking collectives: 0 us -> 41.2 us
  local copies, waits for them, and re-layouts: 8.77 us -> 2.15 us
    dot_general x14 -> x3, matrix products: 271 us -> 3.34 us  [the longest x2 2.62 us: against(): dots = jnp.einsum('bek,bvk->ev', rows, val, precision=lax.Precision.HIGHEST)]
    psum x1 -> x0, waiting for transfers between devices: 173 us -> none  [per_device(): train_feats, val_local = lax.psum((train_terms, val_terms), 'coord')]
    pallas_call x0 -> x2, Pallas kernels: none -> 151 us  [features(): pl.pallas_call(functools.partial(features_kernel, width, len(sets)), grid...]
    reduce_scatter x0 -> x2, waiting for transfers between devices: none -> 72.1 us  [the longest x1 72.1 us: per_device(): first = lax.psum_scatter(first, 'coord', scatter_dimension=0, tiled=True)]
    psum x0 -> x1, blocking collectives: none -> 35.4 us  [per_device(): dots, train_sq, val_sq = lax.psum((dots, train_sq, val_sq), 'coord')]
    all_gather x1 -> x0, waiting for transfers between devices: 20.5 us -> none  [per_device(): val_feats = lax.all_gather(val_local, 'dp', axis=0, tiled=True)]
    unnamed x12 -> x4, local copies, waits for them, and re-layouts: 8.75 us -> 0.01 us
    all_gather x0 -> x1, blocking collectives: none -> 5.81 us  [per_device(): val = lax.all_gather(first[:, half:], 'dp', axis=1, tiled=True)]
  transfers between devices with their start and end apart: 2 -> 2, of which waited for: 2 -> 1; matrix products, arithmetic and copies ran while one was open for 1% -> 0% of each run, Pallas kernels for 0% -> 29%
where the time goes in v1:
time: 287 us; the launch traced here: 286 us
  Pallas kernels  151 us (53%)
  waiting for transfers between devices  72.1 us (25%)
  blocking collectives  41.2 us (14%)
  between operations  14.1 us (5%)
  matrix products  3.34 us (1%)
    pallas_call x2, Pallas kernels, features(): pl.pallas_call(functools.partial(features_kernel, width, len(sets)), grid...  151 us
    reduce_scatter x1, waiting for transfers between devices, per_device(): first = lax.psum_scatter(first, 'coord', scatter_dimension=0, tiled=True)  72.1 us
    psum x1, blocking collectives, per_device(): dots, train_sq, val_sq = lax.psum((dots, train_sq, val_sq), 'coord')  35.4 us
    all_gather x1, blocking collectives, per_device(): val = lax.all_gather(first[:, half:], 'dp', axis=1, tiled=True)  5.81 us
  transfers between devices with their start and end apart: 2, of which 1 were waited for; matrix products, arithmetic and copies ran while one was open for 0% of the time, Pallas kernels for 29%

profile of v1, /device:TPU:0, one launch (start us, length us, event | category | flops | bytes accessed | tf_op | source)
XLA Modules:
  0.0 286.4 jit_solution(15237543654914178302)
XLA Ops:
  7.2 0.0 reduce-scatter.5.cloned.1.call-start
  7.2 1.3 reshape.11.bins_ref
  8.5 68.5 %shard_map.87 = f32[64,64,128]{2,1,0:T(8,128)} custom-call(s32[1280]{0:T(1024)} %reshape.11.bins_ref, bf16[2,128,256,640]{3,2,1,0:T(8,128)(2,1)} %refs_0_.3, bf16[2,128,256,128]{3,2,1,0:T(8,128)(2,1)} %refs_1_.3, bf16[2,640,128,128]{3,2,1,0:T(8,128)(2,1)} %refs_2_.3), custom_call_target="tpu_custom_call" | custom-call | flops 8053063680 | bytes 92274688 | tf_op jit(solution)/shard_map/pallas_call | solution.py:92
  77.0 0.0 reduce-scatter.5.cloned.1.call-update
  77.1 0.0 copy-start.1
  77.1 0.0 reduce-scatter.3.cloned.1.call-start
  77.1 82.2 %shard_map.86 = f32[64,80,128]{2,1,0:T(8,128)} custom-call(s32[1280]{0:T(1024)} %reshape.11.bins_ref, bf16[2,128,256,640]{3,2,1,0:T(8,128)(2,1)} %refs_0_.3, bf16[2,128,256,128]{3,2,1,0:T(8,128)(2,1)} %refs_1_.3, bf16[2,16,256,640]{3,2,1,0:T(8,128)(2,1)} %refs_2_.2, bf16[2,16,256,128]{3,2,1,0:T(8,128)(2,1)} %refs_3_.1, bf16[2,640,128,128]{3,2,1,0:T(8,128)(2,1)} %refs_2_.3), custom_call_target="tpu_custom_call" | custom-call | flops 10066329600 | bytes 104857600 | tf_op jit(solution)/shard_map/pallas_call | solution.py:92
  159.3 0.0 reduce-scatter.3.cloned.1.call-update
  159.3 0.0 copy-done.1
  159.3 0.1 convert_reduce_fusion
  159.4 0.0 reduce-scatter.5.cloned.1.call-done
  159.5 1.1 multiply_reduce_fusion.1
  160.5 72.1 %reduce-scatter.3.cloned.1.call-done = f32[8,80,128]{2,1,0:T(8,128)} async-done(((f32[64,80,128]{2,1,0:T(8,128)}), f32[8,80,128]{2,1,0:T(8,128)}) %reduce-scatter.3.cloned.1.call-update) | async-done | bytes 327696 | tf_op jit(solution)/shard_map/reduce_scatter | solution.py:118
  232.6 0.8 slice.9
  233.5 5.8 %all_gather.3 = f32[8,64,128]{2,1,0:T(8,128)S(1)} all-gather(f32[8,16,128]{2,1,0:T(8,128)S(1)} %slice.9), channel_id=1, replica_groups=mesh['coord'=8,'dp'=4] {'dp'}, dimensions={1}, use_global_device_ids=true | all-gather | bytes 327680 | tf_op jit(solution)/shard_map/all_gather | solution.py:120
  239.3 0.1 multiply_reduce_fusion
  239.4 1.3 convolution_bitcast_fusion.1
  240.7 1.3 convolution_bitcast_fusion
  242.0 0.1 pad_maximum_fusion
  242.1 1.1 multiply_reduce_fusion.2
  243.2 0.1 pad_maximum_fusion.1
  243.3 35.4 %all-reduce = (f32[128,64]{0,1:T(8,128)S(1)}, f32[64]{0:T(128)S(1)}, f32[128]{0:T(128)S(1)}) all-reduce(f32[128,64]{0,1:T(8,128)S(1)} %pad_maximum_fusion, f32[64]{0:T(128)S(1)} %multiply_reduce_fusion, f32[128]{0:T(128)S(1)} %pad_maximum_fusion.1), channel_id=1, replica_groups=mesh['coord'=8,'dp'=4] {'coord'}, use_global_device_ids=true, to_apply=%region_2.0 | all-reduce | flops 8384 | bytes 67072 | tf_op jit(solution)/shard_map/psum | solution.py:130
  278.7 0.1 multiply_divide_fusion
  278.8 0.0 copy-start
  278.8 0.7 convolution_divide_fusion
  279.6 0.0 copy-done
  (2 shorter events, 0.0 us)
Async XLA Ops:
  7.2 152.3 %reduce-scatter.5.cloned.1.call-start = ((), (), s32[]{:S(2)}) async-start(), calls=%async_computation.3 | async-start | bytes 2359296 | tf_op jit(solution)/shard_map/reduce_scatter | solution.py:119
  77.1 82.3 %copy-start.1 = (s32[64,1]{0,1:T(1,128)S(1)}, s32[64,1]{0,1:T(1,128)}, u32[]{:S(2)}) copy-start(s32[64,1]{0,1:T(1,128)} %param.13) | copy-start | bytes 772
  77.1 155.6 %reduce-scatter.3.cloned.1.call-start = ((), (), s32[]{:S(2)}) async-start(), calls=%async_computation.2 | async-start | bytes 2949120 | tf_op jit(solution)/shard_map/reduce_scatter | solution.py:118
  278.8 0.7 copy-start
Sparse Core Ops, SparseCore 0:
  77.2 70.4 reduce-scatter.4
  159.4 73.1 reduce-scatter.2

commit v2 on v1

--- a/solution.py
+++ b/solution.py
@@ -110,24 +110,43 @@
 
 def per_device(h_train, gout_train, h_val, gout_val, proj, bins, tasks):
     n_train, n_val = h_train.shape[1], h_val.shape[1]
-    half = n_train // 2
-    first = features(
-        bins, proj, [(gout_train, h_train, half, 0), (gout_val, h_val, n_val, 0)]
-    )
-    second = features(bins, proj, [(gout_train, h_train, half, 1)])
-    first = lax.psum_scatter(first, "coord", scatter_dimension=0, tiled=True)
-    second = lax.psum_scatter(second, "coord", scatter_dimension=0, tiled=True)
-    val = lax.all_gather(first[:, half:], "dp", axis=1, tiled=True)
+    half, quarter = n_train // 2, n_train // 4
+    sets = [
+        [(gout_train, h_train, half, 0)],
+        [(gout_train, h_train, quarter, 2), (gout_val, h_val, n_val, 0)],
+        [(gout_train, h_train, quarter, 3)],
+    ]
+    sums = []
+    for group in sets:
+        if sums:
+            bins, _ = lax.optimization_barrier((bins, local))
+        local = features(bins, proj, group)
+        sums.append(local)
+    for i in range(len(sums)):
+        if i:
+            sums[i], sums[i - 1] = lax.optimization_barrier((sums[i], sums[i - 1]))
+        sums[i] = lax.psum_scatter(sums[i], "coord", scatter_dimension=0, tiled=True)
+    val = lax.all_gather(sums[1][:, quarter:], "dp", axis=1, tiled=True)
 
     def against(rows):
         dots = jnp.einsum("bek,bvk->ev", rows, val, precision=lax.Precision.HIGHEST)
         return dots, jnp.sum(rows * rows, axis=(0, 2))
 
-    parts = [against(first[:, :half]), against(second)]
-    val_sq = jnp.sum(val * val, axis=(0, 2))
+    parts = [against(rows) for rows in (sums[0], sums[1][:, :quarter], sums[2])]
     dots = jnp.concatenate([p[0] for p in parts], axis=0)
     train_sq = jnp.concatenate([p[1] for p in parts], axis=0)
-    dots, train_sq, val_sq = lax.psum((dots, train_sq, val_sq), "coord")
+    val_sq = jnp.sum(val * val, axis=(0, 2))
+    n_all = dots.shape[1]
+    lanes = -(-(n_all + 1) // 128) * 128
+    packed = jnp.concatenate([dots, train_sq[:, None]], axis=1)
+    packed = jnp.pad(packed, ((0, 8), (0, lanes - n_all - 1)))
+    packed = packed + jnp.pad(val_sq[None, :], ((n_train, 7), (0, lanes - n_all)))
+    packed = jnp.sum(lax.all_gather(packed, "coord", axis=0), axis=0)
+    dots, train_sq, val_sq = (
+        packed[:n_train, :n_all],
+        packed[:n_train, n_all],
+        packed[n_train, :n_all],
+    )
     train_norm = jnp.sqrt(train_sq + 1e-06)
     val_norm = jnp.sqrt(val_sq + 1e-06)
     cosines = dots / (train_norm[:, None] * val_norm[None, :])

time: 287 us -> 325 us (1.13)
  Pallas kernels: 151 us -> 181 us
  waiting for transfers between devices: 72.1 us -> 82.2 us
  blocking collectives: 41.2 us -> 37.4 us
    psum x1 -> x0, blocking collectives: 35.4 us -> none  [per_device(): dots, train_sq, val_sq = lax.psum((dots, train_sq, val_sq), 'coord')]
    all_gather x1 -> x2, blocking collectives: 5.81 us -> 37.4 us  [the longest x1 31.6 us: per_device(): packed = jnp.sum(lax.all_gather(packed, 'coord', axis=0), axis=0)]
    pallas_call x2 -> x3, Pallas kernels: 151 us -> 181 us  [features(): pl.pallas_call(functools.partial(features_kernel, width, len(sets)), grid...]
    reduce_scatter x2 -> x3, waiting for transfers between devices: 72.1 us -> 82.1 us  [per_device(): lax.psum_scatter(sums[i], 'coord', scatter_dimension=0, tiled=True)]
  transfers between devices with their start and end apart: 2 -> 3, of which waited for: 1 -> 3; matrix products, arithmetic and copies ran while one was open for 0% -> 2% of each run, Pallas kernels for 29% -> 34%
where the time goes in v2:
time: 325 us
  Pallas kernels  181 us (56%)
  waiting for transfers between devices  82.2 us (25%)
  blocking collectives  37.4 us (12%)
  between operations  13.8 us (4%)
  local copies, waits for them, and re-layouts  4.27 us (1%)
  matrix products  3.65 us (1%)
    pallas_call x3, Pallas kernels, features(): pl.pallas_call(functools.partial(features_kernel, width, len(sets)), grid...  181 us
    reduce_scatter x3, waiting for transfers between devices, per_device(): lax.psum_scatter(sums[i], 'coord', scatter_dimension=0, tiled=True)  82.1 us
    all_gather x1, blocking collectives, per_device(): packed = jnp.sum(lax.all_gather(packed, 'coord', axis=0), axis=0)  31.6 us
  transfers between devices with their start and end apart: 3, of which 3 were waited for; matrix products, arithmetic and copies ran while one was open for 2% of the time, Pallas kernels for 34%

profile of v2, /device:TPU:0, one launch (start us, length us, event | category | flops | bytes accessed | tf_op | source)
XLA Modules:
  0.0 325.0 jit_solution(3719969119389114763)
XLA Ops:
  7.2 0.0 reduce-scatter.4.cloned.1.call-start
  7.2 1.3 reshape.14.bins_ref
  8.5 0.0 copy-start.1
  8.5 68.7 %shard_map.86 = f32[64,64,128]{2,1,0:T(8,128)} custom-call(s32[1280]{0:T(1024)} %reshape.14.bins_ref, bf16[2,128,256,640]{3,2,1,0:T(8,128)(2,1)} %refs_0_.5, bf16[2,128,256,128]{3,2,1,0:T(8,128)(2,1)} %refs_1_.5, bf16[2,640,128,128]{3,2,1,0:T(8,128)(2,1)} %refs_2_.5), custom_call_target="tpu_custom_call" | custom-call | flops 8053063680 | bytes 92274688 | tf_op jit(solution)/shard_map/pallas_call | solution.py:92
  77.2 0.0 reduce-scatter.4.cloned.1.call-update
  77.2 0.0 reduce-scatter.6.cloned.1.call-start
  77.3 0.0 copy-done.1
  77.3 0.6 reshape.15.bins_ref
  77.9 62.5 %shard_map.87 = f32[64,48,128]{2,1,0:T(8,128)} custom-call(s32[1280]{0:T(1024)} %reshape.15.bins_ref, bf16[2,128,256,640]{3,2,1,0:T(8,128)(2,1)} %refs_0_.5, bf16[2,128,256,128]{3,2,1,0:T(8,128)(2,1)} %refs_1_.5, bf16[2,16,256,640]{3,2,1,0:T(8,128)(2,1)} %refs_2_.4, bf16[2,16,256,128]{3,2,1,0:T(8,128)(2,1)} %refs_3_.1, bf16[2,640,128,128]{3,2,1,0:T(8,128)(2,1)} %refs_2_.5), custom_call_target="tpu_custom_call" | custom-call | flops 6039797760 | bytes 79691776 | tf_op jit(solution)/shard_map/pallas_call | solution.py:92
  140.3 8.0 %reduce-scatter.4.cloned.1.call-done = f32[8,64,128]{2,1,0:T(8,128)} async-done(((f32[64,64,128]{2,1,0:T(8,128)}), f32[8,64,128]{2,1,0:T(8,128)}) %reduce-scatter.4.cloned.1.call-update) | async-done | bytes 262160 | tf_op jit(solution)/shard_map/reduce_scatter | solution.py:128
  148.4 0.0 reduce-scatter.6.cloned.1.call-update
  148.4 0.0 reduce-scatter.8.cloned.1.call-start
  148.4 0.6 reshape.16.bins_ref
  149.1 0.0 copy-start.2
  149.1 0.0 copy-start
  149.1 49.5 %shard_map.88 = f32[64,32,128]{2,1,0:T(8,128)} custom-call(s32[1280]{0:T(1024)} %reshape.16.bins_ref, bf16[2,128,256,640]{3,2,1,0:T(8,128)(2,1)} %refs_0_.5, bf16[2,128,256,128]{3,2,1,0:T(8,128)(2,1)} %refs_1_.5, bf16[2,640,128,128]{3,2,1,0:T(8,128)(2,1)} %refs_2_.5), custom_call_target="tpu_custom_call" | custom-call | flops 4026531840 | bytes 67108864 | tf_op jit(solution)/shard_map/pallas_call | solution.py:92
  198.6 17.3 %reduce-scatter.6.cloned.1.call-done = f32[8,48,128]{2,1,0:T(8,128)} async-done(((f32[64,48,128]{2,1,0:T(8,128)}), f32[8,48,128]{2,1,0:T(8,128)}) %reduce-scatter.6.cloned.1.call-update) | async-done | bytes 196624 | tf_op jit(solution)/shard_map/reduce_scatter | solution.py:128
  216.0 0.0 reduce-scatter.8.cloned.1.call-update
  216.0 0.0 copy-done.2
  216.0 0.1 convert_reduce_fusion
  216.1 0.0 copy-done
  216.1 0.1 multiply_reduce_fusion.1
  216.2 0.9 slice.15
  217.1 5.8 %all_gather.9 = f32[8,64,128]{2,1,0:T(8,128)S(1)} all-gather(f32[8,16,128]{2,1,0:T(8,128)S(1)} %slice.15), channel_id=1, replica_groups=mesh['coord'=8,'dp'=4] {'dp'}, dimensions={1}, use_global_device_ids=true | all-gather | bytes 327680 | tf_op jit(solution)/shard_map/all_gather | solution.py:129
  222.9 0.1 multiply_reduce_fusion
  223.0 0.1 copy.28
  223.1 1.0 multiply_reduce_fusion.3
  224.1 1.3 convolution_bitcast_fusion.1
  225.4 0.4 convolution_bitcast_fusion.2
  225.7 56.7 %reduce-scatter.8.cloned.1.call-done = f32[8,32,128]{2,1,0:T(8,128)} async-done(((f32[64,32,128]{2,1,0:T(8,128)}), f32[8,32,128]{2,1,0:T(8,128)}) %reduce-scatter.8.cloned.1.call-update) | async-done | bytes 131088 | tf_op jit(solution)/shard_map/reduce_scatter | solution.py:128
  282.5 1.0 multiply_reduce_fusion.2
  283.5 0.1 maximum_bitcast_fusion
  283.6 1.3 convolution_bitcast_fusion
  284.8 0.1 fusion
  284.9 0.1 copy.29
  285.0 31.6 %all-gather = f32[1088,128]{1,0:T(8,128)S(1)} all-gather(f32[136,128]{1,0:T(8,128)S(1)} %copy.29), channel_id=2, replica_groups=mesh['coord'=8,'dp'=4] {'coord'}, dimensions={0}, use_global_device_ids=true | all-gather | bytes 626688 | tf_op jit(solution)/shard_map/all_gather | solution.py:144
  316.7 0.2 fusion.3
  316.9 0.1 slice_divide_fusion
  317.0 0.7 copy.30
  317.7 0.8 convolution_divide_fusion
  (2 shorter events, 0.0 us)
Async XLA Ops:
  7.2 141.2 %reduce-scatter.4.cloned.1.call-start = ((), (), s32[]{:S(2)}) async-start(), calls=%async_computation.3 | async-start | bytes 2359296 | tf_op jit(solution)/shard_map/reduce_scatter | solution.py:128
  8.5 68.8 %copy-start.1 = (s32[2,640]{1,0:T(2,128)S(1)}, s32[2,640]{1,0:T(2,128)}, u32[]{:S(2)}) copy-start(s32[2,640]{1,0:T(2,128)} %param.12) | copy-start | bytes 15364
  77.2 138.7 %reduce-scatter.6.cloned.1.call-start = ((), (), s32[]{:S(2)}) async-start(), calls=%async_computation.4 | async-start | bytes 1769472 | tf_op jit(solution)/shard_map/reduce_scatter | solution.py:128
  148.4 134.1 %reduce-scatter.8.cloned.1.call-start = ((), (), s32[]{:S(2)}) async-start(), calls=%async_computation.5 | async-start | bytes 1179648 | tf_op jit(solution)/shard_map/reduce_scatter | solution.py:128
  149.1 66.9 %copy-start.2 = (s32[64,1]{0,1:T(1,128)S(1)}, s32[64,1]{0,1:T(1,128)}, u32[]{:S(2)}) copy-start(s32[64,1]{0,1:T(1,128)} %param.13) | copy-start | bytes 772
  149.1 67.1 %copy-start = (f32[8,64,128]{2,1,0:T(8,128)S(1)}, f32[8,64,128]{2,1,0:T(8,128)}, u32[]{:S(2)}) copy-start(f32[8,64,128]{2,1,0:T(8,128)} %reduce-scatter.4.cloned.1.call-done) | copy-start | bytes 786436
Sparse Core Ops, SparseCore 0:
  77.3 71.0 reduce-scatter.3
  151.8 64.1 reduce-scatter.5
  219.8 62.6 reduce-scatter.7
